TPU v7x, 32 devices: a whole 2x2x4 slice. The times are simulated.
32 devices in a mesh: groups: 2 (over x), pool: 16 (over z, y, core).
Axes of the slice: x: 2, y: 2, z: 4, core: 2. Of those that a mesh axis runs over, the one named last changes fastest.
Arguments:
- query_embed: bfloat16 [256, 1024], P(('groups', 'pool')), parts along dimension 0, may hold values from -40 to 40
- key_slab: bfloat16 [8192, 1024], P(('groups', 'pool')), parts along dimension 0, may hold values from -4 to 4
- nbr_owner: int32 [256, 2], P(('groups', 'pool')), parts along dimension 0, may hold values from 0 to 15, all different within a row; in each aligned block of 8 rows (0 to 7, 8 to 15, ...) at most 2 rows name the same one
- nbr_slot: int32 [256, 2], P(('groups', 'pool')), parts along dimension 0, may hold values from 0 to 3
- enc_table: bfloat16 [128, 64, 896], P(('groups', 'pool')), parts along dimension 0, may hold values from -6 to 6
- stretch_queries: bfloat16 [16384, 2048], P(('groups', 'pool')), parts along dimension 0, may hold values from -6 to 6
- kv_weight: bfloat16 [896, 4096], P(None, 'pool'), may hold values from -0.1875 to 0.1875
Outputs:
- retrieval_lse: float32 [256], P(('groups', 'pool')), parts along dimension 0
- cross_mix: bfloat16 [16384, 2048], P(('groups', 'pool')), parts along dimension 0
There are 2 independent parts, one for each index of `groups`. A program takes and returns all parts, laid end to end along the dimension named above; an argument that names none is the same for every part. Nothing has to cross between parts.
Inputs may be any that keep to these rules, and one draw needn't show every extreme that they name: `nbr_owner`: each row names two different owners. Among the rows of one device no owner is named more than 2 times, and in every draw some device names some owner exactly 2 times.
All inputs are finite; a program needn't handle non-finite values.
Results may differ from a plain program's by a relative error of at most 0.0072.
Values may be sent and summed in bfloat16 or wider, within the bound.
A program may use at most 128 MiB of HBM per device.

v0:
```python
import jax
import jax.numpy as jnp
from jax import lax
from jax.sharding import PartitionSpec as P

HEADS = 16
CAP = 2


def joined(part, axis, combine):
    gathered = lax.all_gather(part, axis)

    def take(source):
        return lax.dynamic_index_in_dim(gathered, source, 0, False)

    return lax.fori_loop(
        1, lax.axis_size(axis), lambda source, state: combine(state, take(source)), take(0)
    )


def log_add(first, second):
    larger = jnp.maximum(first, second)
    return larger + jnp.log(jnp.exp(first - larger) + jnp.exp(second - larger))


def request_ranks(owners):
    count = owners.shape[-1]
    same_owner = owners[..., :, None] == owners[..., None, :]
    before = lax.broadcasted_iota(jnp.int32, (count, count), 1) < lax.broadcasted_iota(
        jnp.int32, (count, count), 0
    )
    return jnp.sum((same_owner & before).astype(jnp.int32), axis=-1)


def local(query_embed, key_slab, nbr_owner, nbr_slot, enc_table, stretch_queries, kv_weight):
    pool_size = lax.axis_size("pool")
    my_index = lax.axis_index("pool")
    q_rows = query_embed.shape[0]
    score_scale = query_embed.shape[1] ** (-0.5)
    logits = (
        lax.dot_general(
            lax.all_gather(query_embed, "pool", axis=0, tiled=True),
            key_slab,
            (((1,), (1,)), ((), ())),
            preferred_element_type=jnp.float32,
        )
        * score_scale
    )
    local_top = jnp.max(logits, axis=1, keepdims=True)
    partials = local_top[:, 0] + jnp.log(jnp.sum(jnp.exp(logits - local_top), axis=1))
    combined = joined(partials, "pool", log_add)
    retrieval_lse = lax.dynamic_slice_in_dim(combined, my_index * q_rows, q_rows)
    table_rows = enc_table.shape[0]
    flat_owner = nbr_owner.reshape(-1)
    flat_slot = nbr_slot.reshape(-1)
    own_ranks = request_ranks(flat_owner)
    target = flat_owner * CAP + own_ranks
    slot_grid = lax.broadcasted_iota(jnp.int32, (1, pool_size * CAP), 1)
    placed = (target[:, None] == slot_grid).astype(jnp.int32)
    slot_table = jnp.sum(placed * (flat_slot[:, None] + 1), axis=0).reshape(pool_size, CAP)
    send_slot_table = lax.all_to_all(slot_table, "pool", split_axis=0, concat_axis=0, tiled=True)
    wanted = jnp.clip(send_slot_table - 1, 0, table_rows - 1)
    filled = (send_slot_table > 0).astype(enc_table.dtype)
    reply = jnp.take(enc_table, wanted, axis=0) * filled[:, :, None, None]
    received = lax.all_to_all(reply, "pool", split_axis=0, concat_axis=0, tiled=True)
    flat_received = received.reshape(pool_size * CAP, received.shape[2], received.shape[3])
    picked = jnp.take(flat_received, target, axis=0)
    enc_rows = picked.reshape(-1, picked.shape[2])
    projected = jnp.dot(
        enc_rows,
        lax.all_gather(kv_weight, "pool", axis=1, tiled=True),
        preferred_element_type=jnp.float32,
    ).astype(jnp.bfloat16)
    width = stretch_queries.shape[1]
    head_dim = width // HEADS
    span = projected.shape[0] // q_rows
    key_part = projected[:, :width].reshape(q_rows, span, HEADS, head_dim)
    value_part = projected[:, width:].reshape(q_rows, span, HEADS, head_dim)
    grouped = stretch_queries.reshape(q_rows, -1, HEADS, head_dim)
    logits = jnp.einsum(
        "cqhd,ckhd->chqk", grouped, key_part, preferred_element_type=jnp.float32
    ) * head_dim ** (-0.5)
    expo = jnp.exp(logits)
    probs = (expo / jnp.sum(expo, axis=-1, keepdims=True)).astype(jnp.bfloat16)
    mixed = jnp.einsum("chqk,ckhd->cqhd", probs, value_part, preferred_element_type=jnp.float32)
    cross_mix = mixed.astype(jnp.bfloat16).reshape(-1, width)
    return (retrieval_lse, cross_mix)


def solution(mesh):
    in_specs = (
        P(("groups", "pool"), None),
        P(("groups", "pool"), None),
        P(("groups", "pool"), None),
        P(("groups", "pool"), None),
        P(("groups", "pool"), None, None),
        P(("groups", "pool"), None),
        P(None, "pool"),
    )
    out_specs = (P(("groups", "pool")), P(("groups", "pool"), None))
    return jax.shard_map(local, mesh=mesh, in_specs=in_specs, out_specs=out_specs, check_vma=False)
```

profile of v0, /device:TPU:0, one launch (start us, length us, event | category | flops | bytes accessed | tf_op | source)
XLA Modules:
  0.0 216.3 jit_solution(18032767880998376728)
XLA Ops:
  7.2 0.7 all-gather.4.cloned.1.call-update
  7.9 0.8 copy.62
  8.8 0.7 broadcast_add_fusion
  9.6 0.2 convert_reduce_fusion
  9.8 0.1 select_reduce_fusion
  10.0 13.6 %all_to_all.14 = s32[16,1,2]{2,1,0:T(1,128)S(1)} all-to-all(s32[16,1,2]{2,1,0:T(1,128)S(1)} %bitcast.78), channel_id=1, replica_groups=mesh['groups'=2,'pool'=16] {'pool'}, dimensions={0} | all-to-all | bytes 256 | tf_op jit(solution)/shard_map/all_to_all | solution.py:61
  23.7 0.1 copy.67
  23.7 0.1 reshape.155
  23.8 0.1 copy.69
  24.0 0.1 copy.66
  24.1 3.9 %gather_fusion = bf16[32,64,896]{2,1,0:T(8,128)(2,1)} fusion(bf16[4,64,896]{2,1,0:T(8,128)(2,1)} %param.13, s32[1024]{0:T(1024)S(1)} %pad_clamp_fusion.1), kind=kCustom, calls=%fused_computation | custom fusion | bytes 7340160 | tf_op jit(solution)/shard_map/jit(_take)/gather | solution.py:64
  28.0 4.5 %select_multiply_fusion = bf16[16,2,64,896]{3,2,1,0:T(8,128)(2,1)} fusion(bf16[16,2,64,896]{3,2,1,0:T(8,128)(2,1)} %bitcast.71, pred[16,2]{1,0:T(8,128)(4,1)S(1)} %copy.66, bf16[16,2]{1,0:T(8,128)(2,1)S(1)} %copy.69), kind=kLoop, calls=%fused_computation.19 | loop fusion | flops 3670016 | bytes 7340128 | tf_op jit(solution)/shard_map/mul | solution.py:64
  32.4 4.7 %all-to-all-start.1 = ((bf16[16,2,64,896]{3,2,1,0:T(8,128)(2,1)}), bf16[16,2,64,896]{3,2,1,0:T(8,128)(2,1)}, u32[]{:S(2)}, u32[]{:S(2)}) async-start(bf16[16,2,64,896]{3,2,1,0:T(8,128)(2,1)} %select_multiply_fusion), calls=%async_computation.1 | async-start | bytes 7340032 | tf_op jit(solution)/shard_map/all_to_all | solution.py:65
  37.4 0.1 broadcast_in_dim.29
  37.5 2.0 copy.76
  39.4 98.2 %all_gather.10 = bf16[128,1024]{1,0:T(8,128)(2,1)S(1)} all-gather(bf16[8,1024]{1,0:T(8,128)(2,1)S(1)} %copy-done.3), channel_id=1, replica_groups=mesh['groups'=2,'pool'=16] {'pool'}, dimensions={0}, use_global_device_ids=true | all-gather | bytes 278528 | tf_op jit(solution)/shard_map/all_gather | solution.py:42
  137.6 0.4 fusion.20
  138.0 0.2 exponential_reduce_fusion
  138.2 41.0 %all-gather.1 = f32[16,1,128]{2,1,0:T(1,128)S(1)} all-gather(f32[1,1,128]{2,1,0:T(1,128)S(1)} %add_bitcast_fusion), channel_id=2, replica_groups=mesh['groups'=2,'pool'=16] {'pool'}, dimensions={0}, use_global_device_ids=true | all-gather | bytes 8704 | tf_op jit(solution)/shard_map/all_gather | solution.py:11
  179.2 0.6 while.15
  179.8 0.6 dynamic_slice.18
  180.4 2.9 %gather_fusion.1 = bf16[16,64,896]{2,1,0:T(8,128)(2,1)S(1)} fusion(bf16[32,64,896]{2,1,0:T(8,128)(2,1)} %bitcast.9, s32[1024]{0:T(1024)S(1)} %pad_clamp_fusion), kind=kCustom, calls=%fused_computation.1 | custom fusion | bytes 3670080 | tf_op jit(solution)/shard_map/jit(_take)/gather | solution.py:67
  183.3 1.8 bitcast_select_fusion
  185.1 11.6 %convolution_convert_fusion = bf16[1024,4096]{1,0:T(8,128)(2,1)S(1)} fusion(bf16[1024,896]{1,0:T(8,128)(2,1)} %bitcast_select_fusion, bf16[896,4096]{1,0:T(8,128)(2,1)} %all-gather.4.cloned.1.call-done), kind=kOutput, calls=%fused_computation.8 | convolution fusion | flops 7520387072 | bytes 17563648 | tf_op jit(solution)/shard_map/dot_general | solution.py:69
  196.8 1.2 slice_bitcast_fusion.1
  198.0 1.4 copy.75
  199.4 1.4 copy.77
  200.8 0.2 copy-done.2
  201.0 3.1 %bitcast_reduce_fusion = (f32[8,16,64]{2,1,0:T(8,128)S(1)}, f32[8,16,128,64]{2,3,1,0:T(8,128)S(1)}) fusion(bf16[8,64,16,128]{3,2,1,0:T(8,128)(2,1)S(1)} %bitcast.76, bf16[8,128,16,128]{3,2,1,0:T(8,128)(2,1)S(1)} %bitcast.73), kind=kOutput, calls=%fused_computation.12 | convolution fusion | flops 270524416 | bytes 10518528 | tf_op jit(solution)/shard_map/cqhd,ckhd->chqk/dot_general | solution.py:80
  204.1 2.2 convert_bitcast_fusion
  206.2 1.4 copy.74
  207.6 1.9 copy.92
  (45 shorter events, 1.2 us)
Async XLA Ops:
  7.2 130.4 %copy-start = (bf16[256,1024]{1,0:T(8,128)(2,1)S(1)}, bf16[256,1024]{1,0:T(8,128)(2,1)}, u32[]{:S(2)}) copy-start(bf16[256,1024]{1,0:T(8,128)(2,1)} %param.10) | copy-start | bytes 1572868
  7.2 177.9 %all-gather.4.cloned.1.call-start = ((), (), s32[]{:S(2)}) async-start(), calls=%async_computation.2 | async-start | bytes 7798784 | tf_op jit(solution)/shard_map/all_gather | solution.py:71
  32.4 4.7 %copy-start.4 = (s32[8,2]{0,1:T(2,128)S(1)}, s32[8,2]{0,1:T(2,128)}, u32[]{:S(2)}) copy-start(s32[8,2]{0,1:T(2,128)} %param.11) | copy-start | bytes 196
  32.4 5.0 %copy-start.1 = (bf16[512,2048]{1,0:T(8,128)(2,1)S(1)}, bf16[512,2048]{1,0:T(8,128)(2,1)}, u32[]{:S(2)}) copy-start(bf16[512,2048]{1,0:T(8,128)(2,1)} %param.14) | copy-start | bytes 6291460
  32.4 148.0 %all-to-all-start.1 = ((bf16[16,2,64,896]{3,2,1,0:T(8,128)(2,1)}), bf16[16,2,64,896]{3,2,1,0:T(8,128)(2,1)}, u32[]{:S(2)}, u32[]{:S(2)}) async-start(bf16[16,2,64,896]{3,2,1,0:T(8,128)(2,1)} %select_multiply_fusion), calls=%async_computation.1 | async-start | bytes 7340032 | tf_op jit(solution)/shard_map/all_to_all | solution.py:65
  37.1 2.3 %copy-start.3 = (bf16[8,1024]{1,0:T(8,128)(2,1)S(1)}, bf16[8,1024]{1,0:T(8,128)(2,1)}, u32[]{:S(2)}) copy-start(bf16[8,1024]{1,0:T(8,128)(2,1)} %param.9) | copy-start | bytes 49156
  199.4 1.6 copy-start.2
Sparse Core Ops, SparseCore 0:
  10.2 127.9 all-gather.3
where the time goes:
time: 217 us; the launch traced here: 216 us
  blocking collectives  153 us (71%)
  local copies, waits for them, and re-layouts  18.6 us (9%)
  matrix products  17.3 us (8%)
  between operations  14.2 us (7%)
  other arithmetic  7.82 us (4%)
  starting transfers between devices  4.7 us (2%)
    all_gather x1, blocking collectives, local(): lax.all_gather(query_embed, 'pool', axis=0, tiled=True)  98.2 us
    all_gather x1, blocking collectives, joined(): gathered = lax.all_gather(part, axis)  41 us
    all_to_all x1, blocking collectives, local(): lax.all_to_all(slot_table, 'pool', split_axis=0, concat_axis=0, tiled=True)  13.6 us
    dot_general x1, matrix products, local(): jnp.dot(enc_rows, lax.all_gather(kv_weight, 'pool', axis=1, tiled=True),...  11.6 us
    unnamed x16, local copies, waits for them, and re-layouts  8.78 us
    all_to_all x1, starting transfers between devices, local(): lax.all_to_all(reply, 'pool', split_axis=0, concat_axis=0, tiled=True)  4.66 us
    mul x1, other arithmetic, local(): reply = jnp.take(enc_table, wanted, axis=0) * filled[:, :, None, None]  4.47 us
  transfers between devices with their start and end apart: 2, of which 0 were waited for; matrix products, arithmetic and copies ran while one was open for 9% of the time, Pallas kernels for 0%

commit v1 on v0

v1 whole, which is shorter than its diff:
```python
import functools

import jax
import jax.numpy as jnp
from jax import lax
from jax.experimental import pallas as pl
from jax.experimental.pallas import tpu as pltpu
from jax.sharding import PartitionSpec as P

HEADS = 16
MESH = pl.DeviceIdType.MESH
F32 = jnp.float32
BF16 = jnp.bfloat16
NT = (((1,), (1,)), ((), ()))


def attention(queries, keys, values, scale):
    logits = lax.dot_general(queries, keys, NT, preferred_element_type=F32) * scale
    expo = jnp.exp(logits)
    probs = (expo / jnp.sum(expo, axis=-1, keepdims=True)).astype(BF16)
    return jnp.dot(probs, values, preferred_element_type=F32).astype(BF16)


def kernel(
    owner_ref, slot_ref, embed_ref, key_ref, enc_ref, queries_ref, weight_ref,
    lse_ref, mix_ref,
    enc_all, weight_all, embed_own, embed_all, part_out, part_all, rows, queries_own, pair_kv,
    send_sem, local_sem, enc_sem, embed_sem, weight_sem, part_sem,
):
    pool = lax.axis_size("pool")
    x = lax.axis_index("groups")
    me = lax.axis_index("pool")
    z, y, c = me // 4, (me // 2) % 2, me % 2
    table = enc_ref.shape[0]
    quarter = weight_ref.shape[0] // 4
    sites = iter(range(send_sem.shape[0]))
    sends = []
    inner = (z + 1) // 2 == 1

    def at(zz, yy, cc):
        return (zz * 2 + yy) * 2 + cc

    side_y, side_c = at(z, 1 - y, c), at(z, y, 1 - c)
    near, mid = at(z + 1 - 2 * (z % 2), y, c), at(3 - z, y, c)
    z_from = (z + 1 - 2 * (z % 2), 2 - z // 2, 3 - 3 * (z // 2))
    z_to = (at(3 - z, y, c), at(3 * z - 3, y, c), at(3 * z - 3, y, c))
    X = {"groups": 1 - x, "pool": me}

    def to(pool_index):
        return {"groups": x, "pool": pool_index}

    def enc_piece(p):
        return enc_all.at[pl.ds(p * table, table)], enc_sem.at[p]

    def embed_piece(p):
        return embed_all.at[p], embed_sem.at[p]

    def weight_piece(number, p):
        start = pl.multiple_of(number * quarter, quarter)
        return weight_all.at[p, pl.ds(start, quarter)], weight_sem.at[p * 4 + number]

    def send(piece, target, when=None, source=None):
        ref, sem = piece
        index = next(sites)
        copy = pltpu.make_async_remote_copy(
            src_ref=ref if source is None else source, dst_ref=ref, send_sem=send_sem.at[index],
            recv_sem=sem, device_id=target, device_id_type=MESH)
        sends.append((copy, when))
        if when is None:
            copy.start()
        else:
            pl.when(when)(copy.start)

    def arrived(piece):
        ref, sem = piece
        pltpu.make_async_remote_copy(
            src_ref=ref, dst_ref=ref, send_sem=send_sem.at[0], recv_sem=sem, device_id=to(side_c),
            device_id_type=MESH).wait_recv()

    barrier = pltpu.get_barrier_semaphore()
    for step in range(1, pool):
        pl.semaphore_signal(barrier, inc=1, device_id=to((me + step) % pool), device_id_type=MESH)
    pl.semaphore_signal(barrier, inc=1, device_id=X, device_id_type=MESH)

    enc_local = pltpu.make_async_copy(enc_ref, enc_piece(me)[0], local_sem.at[0])
    enc_local.start()
    weight_local = pltpu.make_async_copy(weight_ref, weight_all.at[me], local_sem.at[1])
    weight_local.start()
    queries_local = pltpu.make_async_copy(queries_ref, queries_own, local_sem.at[2])
    queries_local.start()
    embed = embed_ref[...].astype(F32)
    half = embed.shape[1] // 2
    folded = jnp.concatenate([embed[:, :half], embed[:, half:]], axis=0).astype(BF16)
    embed_own[...] = folded
    embed_all[me] = folded
    pl.semaphore_wait(barrier, pool)

    own_a, own_b = x * 2, x * 2 + 1
    other_a, other_b = 2 - x * 2, 3 - x * 2

    def own_weight(number):
        return weight_ref.at[pl.ds(pl.multiple_of(number * quarter, quarter), quarter)]

    b_piece, a_piece = weight_piece(own_b, me), weight_piece(own_a, me)
    send(enc_piece(me), to(near), source=enc_ref)
    send(enc_piece(me), to(mid), inner, source=enc_ref)
    send(b_piece, to(side_y), source=own_weight(own_b))
    send(enc_piece(me), to(side_y), source=enc_ref)
    send(embed_piece(me), to(near), source=embed_own)
    send(embed_piece(me), to(mid), inner, source=embed_own)
    send(embed_piece(me), to(side_y), source=embed_own)
    send(embed_piece(me), to(side_c), source=embed_own)
    send(enc_piece(me), to(side_c), source=enc_ref)
    send(b_piece, to(near), source=own_weight(own_b))
    send(b_piece, to(mid), inner, source=own_weight(own_b))
    send(a_piece, to(near), source=own_weight(own_a))
    send(a_piece, to(mid), inner, source=own_weight(own_a))
    send(a_piece, to(side_y), source=own_weight(own_a))
    for number in range(4):
        send(weight_piece(number, me), to(side_c), source=own_weight(number))

    piece = weight_piece(own_b, side_y)
    arrived(piece)
    send(piece, to(near))
    send(piece, to(mid), inner)
    send(piece, X)
    send(piece, to(side_c))

    def from_y(zz):
        p = at(zz, 1 - y, c)
        arrived(embed_piece(p))
        send(embed_piece(p), to(side_c))
        arrived(enc_piece(p))
        send(enc_piece(p), to(side_c))
        piece = weight_piece(own_a, p)
        arrived(piece)
        send(piece, X)
        send(piece, to(side_c))

    for step in range(3):
        p = at(z_from[step], y, c)
        for piece in (embed_piece(p), enc_piece(p)):
            arrived(piece)
            send(piece, to(z_to[step]), inner)
            send(piece, to(side_y))
            send(piece, to(side_c))
        for yy in (y, 1 - y):
            piece = weight_piece(own_b, at(z_from[step], yy, c))
            arrived(piece)
            send(piece, to(z_to[step]), inner)
            send(piece, X)
            send(piece, to(side_c))
        piece = weight_piece(own_a, p)
        arrived(piece)
        send(piece, to(z_to[step]), inner)
        send(piece, to(side_y))
        send(piece, X)
        send(piece, to(side_c))
        from_y(z if step == 0 else z_from[step - 1])
    from_y(z_from[2])

    for zz in range(4):
        for yy in range(2):
            arrived(embed_piece(at(zz, yy, 1 - c)))
    embeds = embed_all[...].reshape(-1, half)
    first = lax.dot_general(embeds, key_ref[:, :half], NT, preferred_element_type=F32)
    second = lax.dot_general(embeds, key_ref[:, half:], NT, preferred_element_type=F32)
    count = embed.shape[0]
    keys = first.shape[1]
    first = first.reshape(pool, 2 * count, keys)[:, :count]
    second = second.reshape(pool, 2 * count, keys)[:, count:]
    scores = (first + second).reshape(pool * count, keys) * (2 * half) ** (-0.5)
    top = jnp.max(scores, axis=1, keepdims=True)
    part = top + jnp.log(jnp.sum(jnp.exp(scores - top), axis=1, keepdims=True))
    part_out[...] = jnp.broadcast_to(part, (pool * count, 128)).reshape(pool, count, 128)
    part_all[me] = part_out[me]
    for step in range(1, pool):
        d = (me + step) % pool
        copy = pltpu.make_async_remote_copy(
            src_ref=part_out.at[d], dst_ref=part_all.at[me], send_sem=send_sem.at[next(sites)],
            recv_sem=part_sem.at[me], device_id=to(d), device_id_type=MESH)
        copy.start()
        sends.append((copy, None))

    piece = weight_piece(other_b, side_y)
    arrived(piece)
    send(piece, to(side_c))
    for step in range(3):
        for number, yy in ((other_b, y), (other_b, 1 - y), (other_a, y)):
            piece = weight_piece(number, at(z_from[step], yy, c))
            arrived(piece)
            send(piece, to(side_c))
        piece = weight_piece(other_a, at(z if step == 0 else z_from[step - 1], 1 - y, c))
        arrived(piece)
        send(piece, to(side_c))
    piece = weight_piece(other_a, at(z_from[2], 1 - y, c))
    arrived(piece)
    send(piece, to(side_c))

    enc_local.wait()
    weight_local.wait()
    queries_local.wait()
    for zz in range(4):
        for yy in range(2):
            p = at(zz, yy, 1 - c)
            arrived(enc_piece(p))
            for number in range(4):
                arrived(weight_piece(number, p))

    tokens = enc_ref.shape[1]
    picks = owner_ref.shape[1]
    for i in range(count):
        for t in range(picks):
            row = (i * picks + t) * tokens
            rows[row:row + tokens, :] = enc_all[owner_ref[i, t] * table + slot_ref[i, t]]

    width = weight_ref.shape[1]
    head_dim = queries_ref.shape[1] // HEADS
    span = picks * tokens
    stretch = queries_ref.shape[0] // count
    scale = head_dim ** (-0.5)

    def pair(step, carry):
        lane = pl.multiple_of(step * width, width)
        pair_kv[0] = jnp.dot(rows[...], weight_all[step], preferred_element_type=F32).astype(BF16)
        pair_kv[1] = jnp.dot(
            rows[...], weight_all[step + pool // 2], preferred_element_type=F32).astype(BF16)
        for i in range(count):
            q = queries_own[i * stretch:(i + 1) * stretch, pl.ds(lane, width)]
            k = pair_kv[0, i * span:(i + 1) * span]
            v = pair_kv[1, i * span:(i + 1) * span]
            mixed = [
                attention(q[:, h:h + head_dim], k[:, h:h + head_dim], v[:, h:h + head_dim], scale)
                for h in range(0, width, head_dim)
            ]
            mix_ref[i * stretch:(i + 1) * stretch, pl.ds(lane, width)] = jnp.concatenate(mixed, axis=1)
        return carry

    lax.fori_loop(0, pool // 2, pair, 0)

    for step in range(1, pool):
        p = (me + step) % pool
        pltpu.make_async_remote_copy(
            src_ref=part_out.at[0], dst_ref=part_all.at[p], send_sem=send_sem.at[0],
            recv_sem=part_sem.at[p], device_id=to(side_c), device_id_type=MESH).wait_recv()
    parts = part_all[...]
    largest = jnp.max(parts, axis=0)
    lse_ref[...] = largest + jnp.log(jnp.sum(jnp.exp(parts - largest[None]), axis=0))
    for copy, when in sends:
        if when is None:
            copy.wait_send()
        else:
            pl.when(when)(copy.wait_send)


def kernel_local(query_embed, key_slab, nbr_owner, nbr_slot, enc_table, stretch_queries, kv_weight):
    pool = lax.axis_size("pool")
    count, wide = query_embed.shape
    vmem = pl.BlockSpec(memory_space=pltpu.VMEM)
    smem = pl.BlockSpec(memory_space=pltpu.SMEM)
    any_space = pl.BlockSpec(memory_space=pl.ANY)
    dma = pltpu.SemaphoreType.DMA
    found = count * nbr_owner.shape[1] * enc_table.shape[1]
    lse, mix = pl.pallas_call(
        kernel,
        out_shape=(
            jax.ShapeDtypeStruct((count, 128), F32),
            jax.ShapeDtypeStruct(stretch_queries.shape, BF16),
        ),
        in_specs=[smem, smem, vmem, vmem, any_space, any_space, any_space],
        out_specs=(vmem, vmem),
        scratch_shapes=[
            pltpu.VMEM((pool * enc_table.shape[0],) + enc_table.shape[1:], BF16),
            pltpu.VMEM((pool,) + kv_weight.shape, BF16),
            pltpu.VMEM((2 * count, wide // 2), BF16),
            pltpu.VMEM((pool, 2 * count, wide // 2), BF16),
            pltpu.VMEM((pool, count, 128), F32),
            pltpu.VMEM((pool, count, 128), F32),
            pltpu.VMEM((found, enc_table.shape[2]), BF16),
            pltpu.VMEM(stretch_queries.shape, BF16),
            pltpu.VMEM((2, found, kv_weight.shape[1]), BF16),
            dma((130,)),
            dma((3,)),
            dma((pool,)),
            dma((pool,)),
            dma((pool * 4,)),
            dma((pool,)),
        ],
        compiler_params=pltpu.CompilerParams(
            collective_id=0, has_side_effects=True, vmem_limit_bytes=48 * 1024 * 1024),
    )(nbr_owner, nbr_slot, query_embed, key_slab, enc_table, stretch_queries, kv_weight)
    return lse[:, 0], mix


def gathered_local(query_embed, key_slab, nbr_owner, nbr_slot, enc_table, stretch_queries, kv_weight):
    me = lax.axis_index("pool")
    count = query_embed.shape[0]
    scores = lax.dot_general(
        lax.all_gather(query_embed, "pool", axis=0, tiled=True), key_slab, NT,
        preferred_element_type=F32) * query_embed.shape[1] ** (-0.5)
    top = jnp.max(scores, axis=1, keepdims=True)
    part = top[:, 0] + jnp.log(jnp.sum(jnp.exp(scores - top), axis=1))
    parts = lax.dynamic_slice_in_dim(lax.all_gather(part, "pool"), me * count, count, 1)
    largest = jnp.max(parts, axis=0)
    lse = largest + jnp.log(jnp.sum(jnp.exp(parts - largest), axis=0))
    table = lax.all_gather(enc_table, "pool", axis=0, tiled=True)
    wanted = (nbr_owner * enc_table.shape[0] + nbr_slot).reshape(-1)
    rows = jnp.take(table, wanted, axis=0).reshape(-1, enc_table.shape[2])
    projected = jnp.dot(
        rows, lax.all_gather(kv_weight, "pool", axis=1, tiled=True),
        preferred_element_type=F32).astype(BF16)
    width = stretch_queries.shape[1]
    head_dim = width // HEADS
    key_part = projected[:, :width].reshape(count, -1, HEADS, head_dim)
    value_part = projected[:, width:].reshape(count, -1, HEADS, head_dim)
    grouped = stretch_queries.reshape(count, -1, HEADS, head_dim)
    logits = jnp.einsum(
        "cqhd,ckhd->chqk", grouped, key_part, preferred_element_type=F32) * head_dim ** (-0.5)
    expo = jnp.exp(logits)
    probs = (expo / jnp.sum(expo, axis=-1, keepdims=True)).astype(BF16)
    mixed = jnp.einsum("chqk,ckhd->cqhd", probs, value_part, preferred_element_type=F32)
    return lse, mixed.astype(BF16).reshape(-1, width)


def solution(mesh):
    in_specs = (
        P(("groups", "pool"), None),
        P(("groups", "pool"), None),
        P(("groups", "pool"), None),
        P(("groups", "pool"), None),
        P(("groups", "pool"), None, None),
        P(("groups", "pool"), None),
        P(None, "pool"),
    )
    out_specs = (P(("groups", "pool")), P(("groups", "pool"), None))
    routed = mesh.shape["groups"] == 2 and mesh.shape["pool"] == 16
    return jax.shard_map(
        kernel_local if routed else gathered_local, mesh=mesh, in_specs=in_specs, out_specs=out_specs,
        check_vma=False)
```

time: 217 us -> 125 us (0.58)
  blocking collectives: 153 us -> 0 us
  Pallas kernels: 0 us -> 115 us
  matrix products: 17.3 us -> 0 us
  between operations: 14.2 us -> 0.64 us
  local copies, waits for them, and re-layouts: 18.6 us -> 8.84 us
  other arithmetic: 7.82 us -> 0 us
  starting transfers between devices: 4.7 us -> 0 us
    all_gather x2 -> x0, blocking collectives: 139 us -> none  [the longest x1 98.2 us: local(): lax.all_gather(query_embed, 'pool', axis=0, tiled=True)]
    pallas_call x0 -> x1, Pallas kernels: none -> 115 us  [kernel_local(): pl.pallas_call(kernel, out_shape=(jax.ShapeDtypeStruct((count, 128), F32)...]
    dot_general x4 -> x0, matrix products: 17.3 us -> none  [the longest x1 11.6 us: local(): jnp.dot(enc_rows, lax.all_gather(kv_weight, 'pool', axis=1, tiled=True),...]
    all_to_all x1 -> x0, blocking collectives: 13.6 us -> none  [local(): lax.all_to_all(slot_table, 'pool', split_axis=0, concat_axis=0, tiled=True)]
    gather x2 -> x0, local copies, waits for them, and re-layouts: 6.78 us -> none  [the longest x1 3.89 us: local(): reply = jnp.take(enc_table, wanted, axis=0) * filled[:, :, None, None]]
    all_to_all x1 -> x0, starting transfers between devices: 4.66 us -> none  [local(): lax.all_to_all(reply, 'pool', split_axis=0, concat_axis=0, tiled=True)]
    mul x2 -> x0, other arithmetic: 4.47 us -> none  [the longest x1 4.47 us: local(): reply = jnp.take(enc_table, wanted, axis=0) * filled[:, :, None, None]]
    unnamed x16 -> x13, local copies, waits for them, and re-layouts: 8.78 us -> 8.21 us
  transfers between devices with their start and end apart: 2 -> 0, of which waited for: 0 -> 0; matrix products, arithmetic and copies ran while one was open for 9% -> 0% of each run, Pallas kernels for 0% -> 0%
where the time goes in v1:
time: 125 us; the launch traced here: 124 us
  Pallas kernels  115 us (92%)
  local copies, waits for them, and re-layouts  8.84 us (7%)
    pallas_call x1, Pallas kernels, kernel_local(): pl.pallas_call(kernel, out_shape=(jax.ShapeDtypeStruct((count, 128), F32)...  115 us
    unnamed x13, local copies, waits for them, and re-layouts  8.21 us

profile of v1, /device:TPU:0, one launch (start us, length us, event | category | flops | bytes accessed | tf_op | source)
XLA Modules:
  0.0 124.0 jit_solution(13618067635402335102)
XLA Ops:
  0.6 0.8 copy.11.owner_ref
  1.4 0.8 copy.12.slot_ref
  2.1 0.0 copy-start
  2.1 1.6 %copy-done = bf16[512,2048]{1,0:T(8,128)(2,1)S(1)} copy-done((bf16[512,2048]{1,0:T(8,128)(2,1)S(1)}, bf16[512,2048]{1,0:T(8,128)(2,1)}, u32[]{:S(2)}) %copy-start) | copy-done | bytes 2097176
  3.7 0.0 copy-start.1
  3.7 1.0 copy-done.1
  4.8 0.0 copy-start.2
  4.8 1.0 copy-done.2
  5.8 0.0 copy-start.3
  5.8 1.0 copy-done.3
  6.8 0.0 copy-start.4
  6.8 0.7 copy-done.4
  7.5 114.5 %shard_map.86 = (f32[8,128]{1,0:T(8,128)S(1)}, bf16[512,2048]{1,0:T(8,128)(2,1)S(1)}) custom-call(s32[8,2]{1,0:T(8,128)S(1)} %copy.11.owner_ref, s32[8,2]{1,0:T(8,128)S(1)} %copy.12.slot_ref, bf16[8,1024]{1,0:T(8,128)(2,1)S(1)} %copy-done.4, bf16[256,1024]{1,0:T(8,128)(2,1)S(1)} %copy-done.1, bf16[4,64,896]{2,1,0:T(8,128)(2,1)S(1)} %copy-done.2, ...), custom_call_target="tpu_custom_call" | custom-call | tf_op jit(solution)/shard_map/pallas_call | solution.py:264
  122.0 0.6 slice_reduce_fusion
  122.7 1.3 %copy.14 = bf16[512,2048]{1,0:T(8,128)(2,1)} copy(bf16[512,2048]{1,0:T(8,128)(2,1)S(1)} %get-tuple-element.9) | data formatting | bytes 4194304
Async XLA Ops:
  2.1 1.6 %copy-start = (bf16[512,2048]{1,0:T(8,128)(2,1)S(1)}, bf16[512,2048]{1,0:T(8,128)(2,1)}, u32[]{:S(2)}) copy-start(bf16[512,2048]{1,0:T(8,128)(2,1)} %queries_ref.1) | copy-start | bytes 6291460
  3.7 1.0 copy-start.1
  4.8 1.0 copy-start.2
  5.8 1.0 copy-start.3
  6.8 0.7 copy-start.4

commit v2 on v1

--- a/solution.py
+++ b/solution.py
@@ -14,17 +14,10 @@
 NT = (((1,), (1,)), ((), ()))
 
 
-def attention(queries, keys, values, scale):
-    logits = lax.dot_general(queries, keys, NT, preferred_element_type=F32) * scale
-    expo = jnp.exp(logits)
-    probs = (expo / jnp.sum(expo, axis=-1, keepdims=True)).astype(BF16)
-    return jnp.dot(probs, values, preferred_element_type=F32).astype(BF16)
-
-
 def kernel(
-    owner_ref, slot_ref, embed_ref, key_ref, enc_ref, queries_ref, weight_ref,
+    owner_ref, slot_ref, embed_ref, key_hbm, enc_ref, queries_ref, weight_ref,
     lse_ref, mix_ref,
-    enc_all, weight_all, embed_own, embed_all, part_out, part_all, rows, queries_own, pair_kv,
+    enc_all, weight_all, embed_own, embed_all, part_out, part_all, rows, queries_own, pair_kv, key_ref,
     send_sem, local_sem, enc_sem, embed_sem, weight_sem, part_sem,
 ):
     pool = lax.axis_size("pool")
@@ -88,6 +81,8 @@
     weight_local.start()
     queries_local = pltpu.make_async_copy(queries_ref, queries_own, local_sem.at[2])
     queries_local.start()
+    key_local = pltpu.make_async_copy(key_hbm, key_ref, local_sem.at[3])
+    key_local.start()
     embed = embed_ref[...].astype(F32)
     half = embed.shape[1] // 2
     folded = jnp.concatenate([embed[:, :half], embed[:, half:]], axis=0).astype(BF16)
@@ -104,8 +99,8 @@
     b_piece, a_piece = weight_piece(own_b, me), weight_piece(own_a, me)
     send(enc_piece(me), to(near), source=enc_ref)
     send(enc_piece(me), to(mid), inner, source=enc_ref)
+    send(enc_piece(me), to(side_y), source=enc_ref)
     send(b_piece, to(side_y), source=own_weight(own_b))
-    send(enc_piece(me), to(side_y), source=enc_ref)
     send(embed_piece(me), to(near), source=embed_own)
     send(embed_piece(me), to(mid), inner, source=embed_own)
     send(embed_piece(me), to(side_y), source=embed_own)
@@ -119,125 +114,171 @@
     for number in range(4):
         send(weight_piece(number, me), to(side_c), source=own_weight(number))
 
-    piece = weight_piece(own_b, side_y)
-    arrived(piece)
-    send(piece, to(near))
-    send(piece, to(mid), inner)
-    send(piece, X)
-    send(piece, to(side_c))
-
-    def from_y(zz):
-        p = at(zz, 1 - y, c)
-        arrived(embed_piece(p))
-        send(embed_piece(p), to(side_c))
-        arrived(enc_piece(p))
-        send(enc_piece(p), to(side_c))
-        piece = weight_piece(own_a, p)
-        arrived(piece)
-        send(piece, X)
-        send(piece, to(side_c))
-
-    for step in range(3):
+    def table_z(step):
         p = at(z_from[step], y, c)
-        for piece in (embed_piece(p), enc_piece(p)):
+        for piece in (enc_piece(p), embed_piece(p)):
             arrived(piece)
             send(piece, to(z_to[step]), inner)
             send(piece, to(side_y))
             send(piece, to(side_c))
+
+    def table_y(step):
+        p = at((z, *z_from)[step], 1 - y, c)
+        for piece in (enc_piece(p), embed_piece(p)):
+            arrived(piece)
+            send(piece, to(side_c))
+
+    def second_y():
+        piece = weight_piece(own_b, side_y)
+        arrived(piece)
+        send(piece, to(near))
+        send(piece, to(mid), inner)
+        send(piece, X)
+        send(piece, to(side_c))
+
+    def second_z(step):
         for yy in (y, 1 - y):
             piece = weight_piece(own_b, at(z_from[step], yy, c))
             arrived(piece)
             send(piece, to(z_to[step]), inner)
             send(piece, X)
             send(piece, to(side_c))
-        piece = weight_piece(own_a, p)
+
+    def first_z(step):
+        piece = weight_piece(own_a, at(z_from[step], y, c))
         arrived(piece)
         send(piece, to(z_to[step]), inner)
         send(piece, to(side_y))
         send(piece, X)
         send(piece, to(side_c))
-        from_y(z if step == 0 else z_from[step - 1])
-    from_y(z_from[2])
-
-    for zz in range(4):
-        for yy in range(2):
-            arrived(embed_piece(at(zz, yy, 1 - c)))
-    embeds = embed_all[...].reshape(-1, half)
-    first = lax.dot_general(embeds, key_ref[:, :half], NT, preferred_element_type=F32)
-    second = lax.dot_general(embeds, key_ref[:, half:], NT, preferred_element_type=F32)
-    count = embed.shape[0]
-    keys = first.shape[1]
-    first = first.reshape(pool, 2 * count, keys)[:, :count]
-    second = second.reshape(pool, 2 * count, keys)[:, count:]
-    scores = (first + second).reshape(pool * count, keys) * (2 * half) ** (-0.5)
-    top = jnp.max(scores, axis=1, keepdims=True)
-    part = top + jnp.log(jnp.sum(jnp.exp(scores - top), axis=1, keepdims=True))
-    part_out[...] = jnp.broadcast_to(part, (pool * count, 128)).reshape(pool, count, 128)
-    part_all[me] = part_out[me]
-    for step in range(1, pool):
-        d = (me + step) % pool
-        copy = pltpu.make_async_remote_copy(
-            src_ref=part_out.at[d], dst_ref=part_all.at[me], send_sem=send_sem.at[next(sites)],
-            recv_sem=part_sem.at[me], device_id=to(d), device_id_type=MESH)
-        copy.start()
-        sends.append((copy, None))
-
-    piece = weight_piece(other_b, side_y)
-    arrived(piece)
-    send(piece, to(side_c))
-    for step in range(3):
-        for number, yy in ((other_b, y), (other_b, 1 - y), (other_a, y)):
-            piece = weight_piece(number, at(z_from[step], yy, c))
-            arrived(piece)
-            send(piece, to(side_c))
-        piece = weight_piece(other_a, at(z if step == 0 else z_from[step - 1], 1 - y, c))
+
+    def first_y(step):
+        piece = weight_piece(own_a, at((z, *z_from)[step], 1 - y, c))
+        arrived(piece)
+        send(piece, X)
+        send(piece, to(side_c))
+
+    def over_x(number, zz, yy):
+        piece = weight_piece(number, at(zz, yy, c))
         arrived(piece)
         send(piece, to(side_c))
-    piece = weight_piece(other_a, at(z_from[2], 1 - y, c))
-    arrived(piece)
-    send(piece, to(side_c))
-
-    enc_local.wait()
-    weight_local.wait()
-    queries_local.wait()
-    for zz in range(4):
-        for yy in range(2):
-            p = at(zz, yy, 1 - c)
-            arrived(enc_piece(p))
-            for number in range(4):
-                arrived(weight_piece(number, p))
+
+    def over_x_z(step):
+        for number, yy in ((other_b, y), (other_b, 1 - y), (other_a, y)):
+            over_x(number, z_from[step], yy)
+
+    def over_x_y(step):
+        over_x(other_a, (z, *z_from)[step], 1 - y)
 
     tokens = enc_ref.shape[1]
     picks = owner_ref.shape[1]
-    for i in range(count):
-        for t in range(picks):
-            row = (i * picks + t) * tokens
-            rows[row:row + tokens, :] = enc_all[owner_ref[i, t] * table + slot_ref[i, t]]
-
+    count = embed.shape[0]
     width = weight_ref.shape[1]
     head_dim = queries_ref.shape[1] // HEADS
     span = picks * tokens
     stretch = queries_ref.shape[0] // count
     scale = head_dim ** (-0.5)
 
-    def pair(step, carry):
-        lane = pl.multiple_of(step * width, width)
-        pair_kv[0] = jnp.dot(rows[...], weight_all[step], preferred_element_type=F32).astype(BF16)
+    def scores():
+        for zz in range(4):
+            for yy in range(2):
+                arrived(embed_piece(at(zz, yy, 1 - c)))
+        key_local.wait()
+        embeds = embed_all[...].reshape(-1, half)
+        first = lax.dot_general(embeds, key_ref[:, :half], NT, preferred_element_type=F32)
+        second = lax.dot_general(embeds, key_ref[:, half:], NT, preferred_element_type=F32)
+        keys = first.shape[1]
+        first = first.reshape(pool, 2 * count, keys)[:, :count]
+        second = second.reshape(pool, 2 * count, keys)[:, count:]
+        both = (first + second).reshape(pool * count, keys) * (2 * half) ** (-0.5)
+        top = jnp.max(both, axis=1, keepdims=True)
+        part = top + jnp.log(jnp.sum(jnp.exp(both - top), axis=1, keepdims=True))
+        part_out[...] = jnp.broadcast_to(part, (pool * count, 128)).reshape(pool, count, 128)
+        part_all[me] = part_out[me]
+        for step in range(1, pool):
+            d = (me + step) % pool
+            copy = pltpu.make_async_remote_copy(
+                src_ref=part_out.at[d], dst_ref=part_all.at[me], send_sem=send_sem.at[next(sites)],
+                recv_sem=part_sem.at[me], device_id=to(d), device_id_type=MESH)
+            copy.start()
+            sends.append((copy, None))
+
+    def pick():
+        enc_local.wait()
+        for zz in range(4):
+            for yy in range(2):
+                arrived(enc_piece(at(zz, yy, 1 - c)))
+        for i in range(count):
+            for t in range(picks):
+                row = (i * picks + t) * tokens
+                rows[row:row + tokens, :] = enc_all[owner_ref[i, t] * table + slot_ref[i, t]]
+
+    def pair(zz, yy, cc):
+        number = at(zz, yy, cc)
+        lane = pl.multiple_of(number * width, width)
+        pair_kv[0] = jnp.dot(rows[...], weight_all[number], preferred_element_type=F32).astype(BF16)
         pair_kv[1] = jnp.dot(
-            rows[...], weight_all[step + pool // 2], preferred_element_type=F32).astype(BF16)
+            rows[...], weight_all[number + pool // 2], preferred_element_type=F32).astype(BF16)
+        zeros = jnp.zeros((stretch, head_dim), BF16)
+        logits = []
         for i in range(count):
             q = queries_own[i * stretch:(i + 1) * stretch, pl.ds(lane, width)]
-            k = pair_kv[0, i * span:(i + 1) * span]
-            v = pair_kv[1, i * span:(i + 1) * span]
-            mixed = [
-                attention(q[:, h:h + head_dim], k[:, h:h + head_dim], v[:, h:h + head_dim], scale)
-                for h in range(0, width, head_dim)
-            ]
-            mix_ref[i * stretch:(i + 1) * stretch, pl.ds(lane, width)] = jnp.concatenate(mixed, axis=1)
-        return carry
-
-    lax.fori_loop(0, pool // 2, pair, 0)
-
+            q = jnp.concatenate([
+                jnp.concatenate([q[:, :head_dim], zeros], axis=1),
+                jnp.concatenate([zeros, q[:, head_dim:]], axis=1)], axis=0)
+            logits.append(lax.dot_general(
+                q, pair_kv[0, i * span:(i + 1) * span], NT, preferred_element_type=F32) * scale)
+        probs = []
+        for block in logits:
+            expo = jnp.exp(block)
+            probs.append((expo / jnp.sum(expo, axis=-1, keepdims=True)).astype(BF16))
+        for i in range(count):
+            mixed = jnp.dot(
+                probs[i], pair_kv[1, i * span:(i + 1) * span], preferred_element_type=F32)
+            mix_ref[i * stretch:(i + 1) * stretch, pl.ds(lane, width)] = jnp.concatenate(
+                [mixed[:stretch, :head_dim], mixed[stretch:, head_dim:]], axis=1).astype(BF16)
+
+    def other_core(zz):
+        for yy in range(2):
+            for source in (at(zz, yy, 1 - c), at(zz + 2, yy, 1 - c)):
+                for number in range(4):
+                    arrived(weight_piece(number, source))
+
+    def pairs(zz, low):
+        def body(step, carry):
+            pair(zz, step % 2, (c + step // 2) % 2)
+            return carry
+
+        lax.fori_loop(low, low + 2, body, 0)
+
+    near_z, far_z = z // 2, 1 - z // 2
+    second_y()
+    for step in range(3):
+        table_z(step)
+        first_z(step)
+        second_z(step)
+        table_y(step)
+        first_y(step)
+        if step == 0:
+            over_x(other_b, z, 1 - y)
+        else:
+            over_x_z(step - 1)
+            over_x_y(step - 1)
+    table_y(3)
+    scores()
+    first_y(3)
+    pick()
+    weight_local.wait()
+    queries_local.wait()
+    over_x_y(2)
+    pairs(near_z, 0)
+    over_x_z(2)
+    other_core(near_z)
+    pairs(near_z, 2)
+    over_x_y(3)
+    pairs(far_z, 0)
+    other_core(far_z)
+    pairs(far_z, 2)
     for step in range(1, pool):
         p = (me + step) % pool
         pltpu.make_async_remote_copy(
@@ -258,7 +299,7 @@
     count, wide = query_embed.shape
     vmem = pl.BlockSpec(memory_space=pltpu.VMEM)
     smem = pl.BlockSpec(memory_space=pltpu.SMEM)
-    any_space = pl.BlockSpec(memory_space=pl.ANY)
+    hbm = pl.BlockSpec(memory_space=pltpu.HBM)
     dma = pltpu.SemaphoreType.DMA
     found = count * nbr_owner.shape[1] * enc_table.shape[1]
     lse, mix = pl.pallas_call(
@@ -267,7 +308,7 @@
             jax.ShapeDtypeStruct((count, 128), F32),
             jax.ShapeDtypeStruct(stretch_queries.shape, BF16),
         ),
-        in_specs=[smem, smem, vmem, vmem, any_space, any_space, any_space],
+        in_specs=[smem, smem, vmem, hbm, hbm, hbm, hbm],
         out_specs=(vmem, vmem),
         scratch_shapes=[
             pltpu.VMEM((pool * enc_table.shape[0],) + enc_table.shape[1:], BF16),
@@ -279,15 +320,16 @@
             pltpu.VMEM((found, enc_table.shape[2]), BF16),
             pltpu.VMEM(stretch_queries.shape, BF16),
             pltpu.VMEM((2, found, kv_weight.shape[1]), BF16),
+            pltpu.VMEM(key_slab.shape, BF16),
             dma((130,)),
-            dma((3,)),
+            dma((4,)),
             dma((pool,)),
             dma((pool,)),
             dma((pool * 4,)),
             dma((pool,)),
         ],
         compiler_params=pltpu.CompilerParams(
-            collective_id=0, has_side_effects=True, vmem_limit_bytes=48 * 1024 * 1024),
+            collective_id=0, has_side_effects=True, vmem_limit_bytes=62 * 1024 * 1024),
     )(nbr_owner, nbr_slot, query_embed, key_slab, enc_table, stretch_queries, kv_weight)
     return lse[:, 0], mix
 
@@ -305,7 +347,8 @@
     lse = largest + jnp.log(jnp.sum(jnp.exp(parts - largest), axis=0))
     table = lax.all_gather(enc_table, "pool", axis=0, tiled=True)
     wanted = (nbr_owner * enc_table.shape[0] + nbr_slot).reshape(-1)
-    rows = jnp.take(table, wanted, axis=0).reshape(-1, enc_table.shape[2])
+    rows = jnp.concatenate(
+        [lax.dynamic_index_in_dim(table, wanted[i], 0, False) for i in range(wanted.shape[0])], axis=0)
     projected = jnp.dot(
         rows, lax.all_gather(kv_weight, "pool", axis=1, tiled=True),
         preferred_element_type=F32).astype(BF16)

time: 125 us -> 95.9 us (0.77)
  Pallas kernels: 115 us -> 87.8 us
  local copies, waits for them, and re-layouts: 8.84 us -> 7.15 us
    pallas_call x1, Pallas kernels: 115 us -> 87.8 us  [kernel_local(): pl.pallas_call(kernel, out_shape=(jax.ShapeDtypeStruct((count, 128), F32)...]
    unnamed x13 -> x3, local copies, waits for them, and re-layouts: 8.21 us -> 5.85 us
where the time goes in v2:
time: 95.9 us; the launch traced here: 95.6 us
  Pallas kernels  87.8 us (92%)
  local copies, waits for them, and re-layouts  7.15 us (7%)
    pallas_call x1, Pallas kernels, kernel_local(): pl.pallas_call(kernel, out_shape=(jax.ShapeDtypeStruct((count, 128), F32)...  87.8 us
    unnamed x3, local copies, waits for them, and re-layouts  5.85 us

profile of v2, /device:TPU:0, one launch (start us, length us, event | category | flops | bytes accessed | tf_op | source)
XLA Modules:
  0.0 95.6 jit_solution(8977826389498023437)
XLA Ops:
  0.6 1.3 %copy.11.owner_ref = s32[8,2]{1,0:T(8,128)} copy(s32[8,2]{0,1:T(2,128)} %param.9) | data formatting | bytes 128 | tf_op args[2]
  2.0 1.3 %copy.12.slot_ref = s32[8,2]{1,0:T(8,128)} copy(s32[8,2]{0,1:T(2,128)} %param.10) | data formatting | bytes 128 | tf_op args[3]
  3.3 87.8 %shard_map.86 = (f32[8,128]{1,0:T(8,128)}, bf16[512,2048]{1,0:T(8,128)(2,1)}) custom-call(s32[8,2]{1,0:T(8,128)} %copy.11.owner_ref, s32[8,2]{1,0:T(8,128)} %copy.12.slot_ref, bf16[8,1024]{1,0:T(8,128)(2,1)} %embed_ref.1, bf16[256,1024]{1,0:T(8,128)(2,1)} %key_hbm.1, bf16[4,64,896]{2,1,0:T(8,128)(2,1)} %enc_ref.1, bf16[512,2048]{1,0:T(8,128)(2,1)} %queries_ref.1, ...), custom_call_target="tpu_custom_call" | custom-call | tf_op jit(solution)/shard_map/pallas_call | solution.py:305
  91.1 1.3 %slice_reduce_fusion = f32[8]{0:T(128)} fusion(f32[8,128]{1,0:T(8,128)} %get-tuple-element.4), kind=kLoop, calls=%fused_computation | loop fusion | bytes 64 | tf_op jit(solution)/shard_map/slice | solution.py:334
  92.4 3.2 %copy.14 = bf16[512,2048]{1,0:T(8,128)(2,1)} copy(bf16[512,2048]{1,0:T(8,128)(2,1)} %get-tuple-element.9) | data formatting | bytes 4194304

commit v3 on v2

--- a/solution.py
+++ b/solution.py
@@ -42,8 +42,8 @@
     def to(pool_index):
         return {"groups": x, "pool": pool_index}
 
-    def enc_piece(p):
-        return enc_all.at[pl.ds(p * table, table)], enc_sem.at[p]
+    def enc_piece(p, entry):
+        return enc_all.at[p * table + entry], enc_sem.at[p * table + entry]
 
     def embed_piece(p):
         return embed_all.at[p], embed_sem.at[p]
@@ -75,7 +75,7 @@
         pl.semaphore_signal(barrier, inc=1, device_id=to((me + step) % pool), device_id_type=MESH)
     pl.semaphore_signal(barrier, inc=1, device_id=X, device_id_type=MESH)
 
-    enc_local = pltpu.make_async_copy(enc_ref, enc_piece(me)[0], local_sem.at[0])
+    enc_local = pltpu.make_async_copy(enc_ref, enc_all.at[pl.ds(me * table, table)], local_sem.at[0])
     enc_local.start()
     weight_local = pltpu.make_async_copy(weight_ref, weight_all.at[me], local_sem.at[1])
     weight_local.start()
@@ -97,36 +97,51 @@
         return weight_ref.at[pl.ds(pl.multiple_of(number * quarter, quarter), quarter)]
 
     b_piece, a_piece = weight_piece(own_b, me), weight_piece(own_a, me)
-    send(enc_piece(me), to(near), source=enc_ref)
-    send(enc_piece(me), to(mid), inner, source=enc_ref)
-    send(enc_piece(me), to(side_y), source=enc_ref)
+    def own_table(entry):
+        piece, source = enc_piece(me, entry), enc_ref.at[entry]
+        send(piece, to(near), source=source)
+        send(piece, to(mid), inner, source=source)
+        send(piece, to(side_y), source=source)
+        send(piece, to(side_c), source=source)
+
     send(b_piece, to(side_y), source=own_weight(own_b))
+    own_table(0)
     send(embed_piece(me), to(near), source=embed_own)
     send(embed_piece(me), to(mid), inner, source=embed_own)
     send(embed_piece(me), to(side_y), source=embed_own)
     send(embed_piece(me), to(side_c), source=embed_own)
-    send(enc_piece(me), to(side_c), source=enc_ref)
-    send(b_piece, to(near), source=own_weight(own_b))
-    send(b_piece, to(mid), inner, source=own_weight(own_b))
+    own_table(1)
     send(a_piece, to(near), source=own_weight(own_a))
     send(a_piece, to(mid), inner, source=own_weight(own_a))
     send(a_piece, to(side_y), source=own_weight(own_a))
+    own_table(2)
+    send(b_piece, to(near), source=own_weight(own_b))
+    send(b_piece, to(mid), inner, source=own_weight(own_b))
+    own_table(3)
     for number in range(4):
         send(weight_piece(number, me), to(side_c), source=own_weight(number))
 
-    def table_z(step):
-        p = at(z_from[step], y, c)
-        for piece in (enc_piece(p), embed_piece(p)):
-            arrived(piece)
-            send(piece, to(z_to[step]), inner)
-            send(piece, to(side_y))
-            send(piece, to(side_c))
-
-    def table_y(step):
-        p = at((z, *z_from)[step], 1 - y, c)
-        for piece in (enc_piece(p), embed_piece(p)):
-            arrived(piece)
-            send(piece, to(side_c))
+    def hand_z(piece, step):
+        arrived(piece)
+        send(piece, to(z_to[step]), inner)
+        send(piece, to(side_y))
+        send(piece, to(side_c))
+
+    def hand_y(piece):
+        arrived(piece)
+        send(piece, to(side_c))
+
+    def table_z(step, entry):
+        hand_z(enc_piece(at(z_from[step], y, c), entry), step)
+
+    def table_y(step, entry):
+        hand_y(enc_piece(at((z, *z_from)[step], 1 - y, c), entry))
+
+    def embed_z(step):
+        hand_z(embed_piece(at(z_from[step], y, c)), step)
+
+    def embed_y(step):
+        hand_y(embed_piece(at((z, *z_from)[step], 1 - y, c)))
 
     def second_y():
         piece = weight_piece(own_b, side_y)
@@ -136,13 +151,12 @@
         send(piece, X)
         send(piece, to(side_c))
 
-    def second_z(step):
-        for yy in (y, 1 - y):
-            piece = weight_piece(own_b, at(z_from[step], yy, c))
-            arrived(piece)
-            send(piece, to(z_to[step]), inner)
-            send(piece, X)
-            send(piece, to(side_c))
+    def second_z(step, yy):
+        piece = weight_piece(own_b, at(z_from[step], yy, c))
+        arrived(piece)
+        send(piece, to(z_to[step]), inner)
+        send(piece, X)
+        send(piece, to(side_c))
 
     def first_z(step):
         piece = weight_piece(own_a, at(z_from[step], y, c))
@@ -171,7 +185,7 @@
         over_x(other_a, (z, *z_from)[step], 1 - y)
 
     tokens = enc_ref.shape[1]
-    picks = owner_ref.shape[1]
+    picks = owner_ref.shape[0]
     count = embed.shape[0]
     width = weight_ref.shape[1]
     head_dim = queries_ref.shape[1] // HEADS
@@ -207,11 +221,12 @@
         enc_local.wait()
         for zz in range(4):
             for yy in range(2):
-                arrived(enc_piece(at(zz, yy, 1 - c)))
+                for entry in range(table):
+                    arrived(enc_piece(at(zz, yy, 1 - c), entry))
         for i in range(count):
             for t in range(picks):
                 row = (i * picks + t) * tokens
-                rows[row:row + tokens, :] = enc_all[owner_ref[i, t] * table + slot_ref[i, t]]
+                rows[row:row + tokens, :] = enc_all[owner_ref[t, i] * table + slot_ref[t, i]]
 
     def pair(zz, yy, cc):
         number = at(zz, yy, cc)
@@ -254,17 +269,28 @@
     near_z, far_z = z // 2, 1 - z // 2
     second_y()
     for step in range(3):
-        table_z(step)
+        table_z(step, 0)
+        embed_z(step)
+        table_y(step, 0)
+        embed_y(step)
+        table_z(step, 1)
+        table_y(step, 1)
         first_z(step)
-        second_z(step)
-        table_y(step)
+        table_z(step, 2)
         first_y(step)
+        table_y(step, 2)
+        second_z(step, y)
+        table_z(step, 3)
+        second_z(step, 1 - y)
+        table_y(step, 3)
         if step == 0:
             over_x(other_b, z, 1 - y)
         else:
             over_x_z(step - 1)
             over_x_y(step - 1)
-    table_y(3)
+    embed_y(3)
+    for entry in range(table):
+        table_y(3, entry)
     scores()
     first_y(3)
     pick()
@@ -321,16 +347,16 @@
             pltpu.VMEM(stretch_queries.shape, BF16),
             pltpu.VMEM((2, found, kv_weight.shape[1]), BF16),
             pltpu.VMEM(key_slab.shape, BF16),
-            dma((130,)),
+            dma((190,)),
             dma((4,)),
-            dma((pool,)),
+            dma((pool * enc_table.shape[0],)),
             dma((pool,)),
             dma((pool * 4,)),
             dma((pool,)),
         ],
         compiler_params=pltpu.CompilerParams(
             collective_id=0, has_side_effects=True, vmem_limit_bytes=62 * 1024 * 1024),
-    )(nbr_owner, nbr_slot, query_embed, key_slab, enc_table, stretch_queries, kv_weight)
+    )(nbr_owner.T, nbr_slot.T, query_embed, key_slab, enc_table, stretch_queries, kv_weight)
     return lse[:, 0], mix
 
 

time: 95.9 us -> 90 us (0.938)
  Pallas kernels: 87.8 us -> 84.4 us
  local copies, waits for them, and re-layouts: 7.15 us -> 4.47 us
    pallas_call x1, Pallas kernels: 87.8 us -> 84.4 us  [kernel_local(): pl.pallas_call(kernel, out_shape=(jax.ShapeDtypeStruct((count, 128), F32)...]
    unnamed x3 -> x1, local copies, waits for them, and re-layouts: 5.85 us -> 3.16 us
where the time goes in v3:
time: 90 us; the launch traced here: 89.5 us
  Pallas kernels  84.4 us (94%)
  local copies, waits for them, and re-layouts  4.47 us (5%)
    pallas_call x1, Pallas kernels, kernel_local(): pl.pallas_call(kernel, out_shape=(jax.ShapeDtypeStruct((count, 128), F32)...  84.4 us
    unnamed x1, local copies, waits for them, and re-layouts  3.16 us

profile of v3, /device:TPU:0, one launch (start us, length us, event | category | flops | bytes accessed | tf_op | source)
XLA Modules:
  0.0 89.5 jit_solution(15966345563871572674)
XLA Ops:
  0.6 84.4 %shard_map.86 = (f32[8,128]{1,0:T(8,128)}, bf16[512,2048]{1,0:T(8,128)(2,1)}) custom-call(s32[2,8]{1,0:T(2,128)} %bitcast.2, s32[2,8]{1,0:T(2,128)} %bitcast.3, bf16[8,1024]{1,0:T(8,128)(2,1)} %embed_ref.1, bf16[256,1024]{1,0:T(8,128)(2,1)} %key_hbm.1, bf16[4,64,896]{2,1,0:T(8,128)(2,1)} %enc_ref.1, bf16[512,2048]{1,0:T(8,128)(2,1)} %queries_ref.1, ...), custom_call_target="tpu_custom_call" | custom-call | tf_op jit(solution)/shard_map/pallas_call | solution.py:331
  85.0 1.3 %slice_reduce_fusion = f32[8]{0:T(128)} fusion(f32[8,128]{1,0:T(8,128)} %get-tuple-element.4), kind=kLoop, calls=%fused_computation | loop fusion | bytes 64 | tf_op jit(solution)/shard_map/slice | solution.py:360
  86.3 3.2 %copy.10 = bf16[512,2048]{1,0:T(8,128)(2,1)} copy(bf16[512,2048]{1,0:T(8,128)(2,1)} %get-tuple-element.9) | data formatting | bytes 4194304
